TPU v7x, 32 devices: a whole 2x2x4 slice. The times are simulated.
32 devices in a mesh: dp: 16 (over z, y, core), ctx: 2 (over x).
Axes of the slice: x: 2, y: 2, z: 4, core: 2. Of those that a mesh axis runs over, the one named last changes fastest.
Arguments:
- frames: bfloat16 [16, 1024, 1280], P('dp', 'ctx'), may hold values from -6 to 6
- conv_taps: float32 [31, 1280], replicated, may hold values from -1 to 1
- conv_gain: float32 [1280], replicated, may hold values from 0.1 to 1.9
- w_kv: bfloat16 [1280, 2560], P('dp'), may hold values from -0.15625 to 0.15625
- queries: bfloat16 [16, 32, 1280], P('dp', 'ctx'), may hold values from -6 to 6
- out_grad: bfloat16 [16, 32, 1280], P('dp', 'ctx'), may hold values from -6 to 6
- frame_len: int32 [16], P('dp'), may hold values from 256 to 1024
- token_len: int32 [16], P('dp'), may hold values from 8 to 32
Outputs:
- frames_grad: bfloat16 [16, 1024, 1280], P('dp', 'ctx')
- taps_grad: float32 [31, 1280], replicated
- gain_grad: float32 [1280], replicated
- w_kv_grad: float32 [1280, 2560], P('dp')
- queries_grad: bfloat16 [16, 32, 1280], P('dp', 'ctx')
Inputs may be any that keep to these rules, and one draw needn't show every extreme that they name: frames at positions of frame_len[b] or beyond are padding of utterance b. Tokens at positions of token_len[b] or beyond are padding of utterance b.
All inputs are finite; a program needn't handle non-finite values.
Results may differ from a plain program's by a relative error of at most 0.012.
Values may be sent and summed in bfloat16 or wider, within the bound.
A program may use at most 128 MiB of HBM per device.

v0:
```python
import jax
import jax.numpy as jnp
from jax import lax
from jax.sharding import PartitionSpec as P

HEADS = 20


def padded_2(block, sides, width):
    for axis, dim in sides:
        count = lax.axis_size(axis)
        forward = [(i, i + 1) for i in range(count - 1)]
        backward = [(target, source) for source, target in forward]
        low = lax.ppermute(
            lax.slice_in_dim(block, block.shape[dim] - width, None, axis=dim), axis, forward
        )
        high = lax.ppermute(lax.slice_in_dim(block, 0, width, axis=dim), axis, backward)
        block = jnp.concatenate([low, block, high], axis=dim)
    return block


def shifted(value, axis, steps):
    count = lax.axis_size(axis)
    pairs = [(source, (source + steps) % count) for source in range(count)]
    return lax.ppermute(value, axis, pairs)


def conv_time(padded, conv_taps, length):
    total = jnp.zeros((length, padded.shape[1]), jnp.float32)
    for tap_idx in range(conv_taps.shape[0]):
        total = total + conv_taps[tap_idx] * padded[tap_idx : tap_idx + length].astype(jnp.float32)
    return total


def silu_slope(gated):
    sigma = jax.nn.sigmoid(gated)
    return sigma * (1.0 + gated * (1.0 - sigma))


def forward_part(query_block, key_block, value_block, live_mask, head_count):
    row_count = query_block.shape[0]
    frame_count = key_block.shape[0]
    q_heads = query_block.reshape(row_count, head_count, -1)
    k_heads = key_block.reshape(frame_count, head_count, -1)
    v_heads = value_block.reshape(frame_count, head_count, -1)
    scale = q_heads.shape[2] ** (-0.5)
    exp_scores = (
        jnp.exp(
            jnp.einsum("thd,fhd->htf", q_heads, k_heads, preferred_element_type=jnp.float32) * scale
        )
        * live_mask
    )
    totals = jnp.sum(exp_scores, axis=2).T
    weighted = jnp.einsum(
        "htf,fhd->thd", exp_scores.astype(jnp.bfloat16), v_heads, preferred_element_type=jnp.float32
    )
    return (weighted.reshape(row_count, -1), totals)


def backward_part(
    query_block, grad_block, totals, delta_rows, key_block, value_block, live_mask, head_count
):
    row_count = query_block.shape[0]
    frame_count = key_block.shape[0]
    q_heads = query_block.reshape(row_count, head_count, -1)
    g_heads = grad_block.reshape(row_count, head_count, -1)
    k_heads = key_block.reshape(frame_count, head_count, -1)
    v_heads = value_block.reshape(frame_count, head_count, -1)
    scale = q_heads.shape[2] ** (-0.5)
    exp_scores = (
        jnp.exp(
            jnp.einsum("thd,fhd->htf", q_heads, k_heads, preferred_element_type=jnp.float32) * scale
        )
        * live_mask
    )
    attn_prob = exp_scores / totals.T[:, :, None]
    d_prob = jnp.einsum("thd,fhd->htf", g_heads, v_heads, preferred_element_type=jnp.float32)
    d_score = (attn_prob * (d_prob - delta_rows.T[:, :, None])).astype(jnp.bfloat16)
    query_part = jnp.einsum(
        "htf,fhd->thd", d_score, k_heads, preferred_element_type=jnp.float32
    ).reshape(row_count, -1)
    key_part = jnp.einsum(
        "htf,thd->fhd", d_score, q_heads, preferred_element_type=jnp.float32
    ).reshape(frame_count, -1)
    value_part = jnp.einsum(
        "htf,thd->fhd", attn_prob.astype(jnp.bfloat16), g_heads, preferred_element_type=jnp.float32
    ).reshape(frame_count, -1)
    return (query_part, key_part, value_part)


def row_delta(weighted, totals, grad_block):
    row_count = weighted.shape[0]
    head_count = totals.shape[1]
    head_dim = weighted.shape[1] // head_count
    attended = weighted / jnp.repeat(totals, head_dim, axis=1)
    return jnp.sum(
        (grad_block.astype(jnp.float32) * attended).reshape(row_count, head_count, head_dim), axis=2
    )


def per_device(frames, conv_taps, conv_gain, w_kv, queries, out_grad, frame_len, token_len):
    cycle_size = lax.axis_size("ctx")
    cycle_pos = lax.axis_index("ctx")
    length = frames.shape[1]
    model_width = frames.shape[2]
    tokens = queries.shape[1]
    tap_count = conv_taps.shape[0]
    rim_width = tap_count // 2
    scale = (model_width // HEADS) ** (-0.5)
    padded = padded_2(frames, (("ctx", 1),), rim_width)[0]
    conv_out = conv_time(padded, conv_taps, length)
    gated = conv_gain * conv_out
    encoded = (frames[0].astype(jnp.float32) + jax.nn.silu(gated)).astype(jnp.bfloat16)
    w_full = lax.all_gather(w_kv, "dp", axis=0, tiled=True)
    key_values = jnp.dot(encoded, w_full, preferred_element_type=jnp.float32).astype(jnp.bfloat16)
    key_block = key_values[:, :model_width]
    value_block = key_values[:, model_width:]
    frame_pos = cycle_pos * length + jnp.arange(length)
    live_mask = (frame_pos < frame_len[0]).astype(jnp.float32)
    token_pos = cycle_pos * tokens + jnp.arange(tokens)
    grad_block = out_grad[0] * (token_pos < token_len[0]).astype(jnp.bfloat16)[:, None]
    query_block = queries[0]

    def forward_tile(visitor, keys_part, values_part, head_count):
        return forward_part(visitor, keys_part, values_part, live_mask, head_count)

    def backward_tile(
        visitor, visit_grad, visit_totals, visit_delta, keys_part, values_part, head_count
    ):
        return backward_part(
            visitor,
            visit_grad,
            visit_totals,
            visit_delta,
            keys_part,
            values_part,
            live_mask,
            head_count,
        )

    def forward_turn(turn_idx, carried):
        visitor, weighted, totals = carried
        part_sum, part_total = forward_tile(visitor, key_block, value_block, HEADS)
        visitor = shifted(visitor, "ctx", 1)
        weighted, totals = shifted((weighted + part_sum, totals + part_total), "ctx", 1)
        return (visitor, weighted, totals)

    first_state = (
        query_block,
        jnp.zeros((tokens, model_width), jnp.float32),
        jnp.zeros((tokens, HEADS), jnp.float32),
    )
    first_out = lax.fori_loop(0, cycle_size, forward_turn, first_state)
    totals = first_out[2]
    delta_rows = row_delta(first_out[1], totals, grad_block)

    def backward_turn(turn_idx, carried):
        visitor, visit_grad, visit_totals, visit_delta, query_acc, key_acc, value_acc = carried
        part_query, part_key, part_value = backward_tile(
            visitor, visit_grad, visit_totals, visit_delta, key_block, value_block, HEADS
        )
        visitor, visit_grad = shifted((visitor, visit_grad), "ctx", 1)
        visit_totals, visit_delta, query_acc = shifted(
            (visit_totals, visit_delta, query_acc + part_query), "ctx", 1
        )
        return (
            visitor,
            visit_grad,
            visit_totals,
            visit_delta,
            query_acc,
            key_acc + part_key,
            value_acc + part_value,
        )

    second_state = (
        query_block,
        grad_block,
        totals,
        delta_rows,
        jnp.zeros((tokens, model_width), jnp.float32),
        jnp.zeros((length, model_width), jnp.float32),
        jnp.zeros((length, model_width), jnp.float32),
    )
    second_out = lax.fori_loop(0, cycle_size, backward_turn, second_state)
    query_acc = second_out[4]
    key_acc = second_out[5]
    value_acc = second_out[6]
    queries_grad = (query_acc * scale).astype(jnp.bfloat16)[None]
    kv_grad = jnp.concatenate([key_acc * scale, value_acc], 1).astype(jnp.bfloat16)
    enc_grad = lax.dot_general(
        kv_grad, w_full, (((1,), (1,)), ((), ())), preferred_element_type=jnp.float32
    )
    gated_grad = enc_grad * silu_slope(gated)
    gain_term = jnp.sum(gated_grad * conv_out, axis=0)
    conv_grad = gated_grad * conv_gain
    tap_terms = jnp.stack(
        [
            jnp.sum(conv_grad * padded[tap_idx : tap_idx + length].astype(jnp.float32), axis=0)
            for tap_idx in range(tap_count)
        ]
    )
    padded_grad = padded_2(conv_grad[None], (("ctx", 1),), rim_width)[0]
    back_conv = jnp.zeros((length, model_width), jnp.float32)
    for tap_idx in range(tap_count):
        offset = 2 * rim_width - tap_idx
        back_conv = back_conv + conv_taps[tap_idx] * padded_grad[offset : offset + length]
    frames_grad = (enc_grad + back_conv).astype(jnp.bfloat16)[None]
    taps_grad, gain_grad = lax.psum((tap_terms, gain_term), ("dp", "ctx"))
    data_part = lax.psum_scatter(
        lax.dot_general(
            encoded, kv_grad, (((0,), (0,)), ((), ())), preferred_element_type=jnp.float32
        ),
        "dp",
        scatter_dimension=0,
        tiled=True,
    )
    w_kv_grad = lax.psum(data_part, "ctx")
    return (frames_grad, taps_grad, gain_grad, w_kv_grad, queries_grad)


def solution(mesh):
    placed = (
        P("dp", "ctx", None),
        P(),
        P(),
        P("dp", None),
        P("dp", "ctx", None),
        P("dp", "ctx", None),
        P("dp"),
        P("dp"),
    )
    return jax.shard_map(
        per_device,
        mesh=mesh,
        in_specs=placed,
        out_specs=(P("dp", "ctx", None), P(), P(), P("dp", None), P("dp", "ctx", None)),
        check_vma=False,
    )
```

profile of v0, /device:TPU:0, one launch (start us, length us, event | category | flops | bytes accessed | tf_op | source)
XLA Modules:
  0.0 496.1 jit_solution(5663490250576671858)
XLA Ops:
  9.6 4.8 collective-permute-start.8
  22.3 12.4 %fusion.82 = (bf16[512,1280]{1,0:T(8,128)(2,1)}, f32[512,1280]{1,0:T(8,128)}) fusion(bf16[1,512,1280]{2,1,0:T(8,128)(2,1)S(1)} %copy-done.4, f32[1280]{0:T(1024)S(1)} %copy-done.75, bf16[1,527,1280]{2,1,0:T(8,128)(2,1)S(1)} %constant_dynamic-update-slice_fusion, f32[1280]{0:T(1024)S(1)} %get-tuple-element.290, f32[1280]{0:T(1024)S(1)} %get-tuple-element.291, ...), kind=kLoop, calls=%fused_computation.196 | loop fusion | flops 104202240 | bytes 25105920 | tf_op jit(solution)/shard_map/convert_element_type | solution.py:113
  35.0 41.4 %all-gather.2.cloned.1.call-done = bf16[1280,2560]{1,0:T(8,128)(2,1)} async-done(((bf16[80,2560]{1,0:T(8,128)(2,1)}), bf16[1280,2560]{1,0:T(8,128)(2,1)}) %all-gather.2.cloned.1.call-update) | async-done | bytes 6553616 | tf_op jit(solution)/shard_map/all_gather | solution.py:114
  76.4 6.8 %convolution_convert_fusion = bf16[512,2560]{1,0:T(8,128)(2,1)S(1)} fusion(bf16[512,1280]{1,0:T(8,128)(2,1)} %get-tuple-element.335, bf16[1280,2560]{1,0:T(8,128)(2,1)} %all-gather.2.cloned.1.call-done), kind=kOutput, calls=%fused_computation.72 | convolution fusion | flops 3356753920 | bytes 10485760 | tf_op jit(solution)/shard_map/dot_general | solution.py:115
  86.6 2.4 copy.42
  89.6 19.6 %while.38 = (s32[]{:T(128)}, bf16[16,1280]{1,0:T(8,128)(2,1)S(1)}, f32[16,1280]{1,0:T(8,128)S(1)}, f32[16,20]{0,1:T(8,128)}, bf16[512,1280]{0,1:T(8,128)(2,1)}, ...) while((s32[]{:T(128)}, bf16[16,1280]{1,0:T(8,128)(2,1)S(1)}, ...), condition=%wide.region_2.3_spmd.clone, body=%wide.region_0.2_spmd.clone.sunk | while | flops 42620416 | bytes 4643037 | solution.py:153
  97.1 2.3 collective-permute-done.2
  112.5 56.3 %while.39 = (s32[]{:T(128)}, bf16[16,1280]{1,0:T(8,128)(2,1)}, bf16[16,1280]{1,0:T(8,128)(2,1)}, f32[16,20]{0,1:T(8,128)}, f32[16,20]{0,1:T(8,128)}, /*index=5*/...) while((s32[]{:T(128)}, bf16[16,1280]{1,0:T(8,128)(2,1)}, ...), condition=%wide.region_5.6_spmd.clone, body=%wide.region_4.5_spmd.clone.sunk | while | flops 108647936 | bytes 37869488 | solution.py:185
  128.3 3.1 fusion.294
  133.5 6.1 %bitcast_add_fusion.6 = (f32[512,1280]{0,1:T(8,128)}, f32[512,1280]{0,1:T(8,128)}) fusion(f32[20,512,64]{1,2,0:T(8,128)} %fusion.294, f32[512,1280]{0,1:T(8,128)} %get-tuple-element.528, pred[]{:T(512)S(6)} %compare.3, f32[20,512,64]{1,2,0:T(8,128)} %fusion.295, f32[512,1280]{0,1:T(8,128)} %get-tuple-element.527), kind=kLoop, calls=%fused_computation.11.clone.1 | loop fusion | flops 2621440 | bytes 15728641 | tf_op jit(solution)/shard_map/while/body/eval_jaxpr/add | solution.py:173
  155.2 3.1 fusion.294
  160.5 7.7 %bitcast_add_fusion.6 = (f32[512,1280]{0,1:T(8,128)}, f32[512,1280]{0,1:T(8,128)}) fusion(f32[20,512,64]{1,2,0:T(8,128)} %fusion.294, f32[512,1280]{0,1:T(8,128)} %get-tuple-element.528, pred[]{:T(512)S(6)} %compare.3, f32[20,512,64]{1,2,0:T(8,128)} %fusion.295, f32[512,1280]{0,1:T(8,128)} %get-tuple-element.527), kind=kLoop, calls=%fused_computation.11.clone.1 | loop fusion | flops 2621440 | bytes 15728641 | tf_op jit(solution)/shard_map/while/body/eval_jaxpr/add | solution.py:173
  172.6 7.7 %fusion.204 = f32[1280,2560]{1,0:T(8,128)} fusion(bf16[512,1280]{1,0:T(8,128)(2,1)S(1)} %copy-done.10, bf16[512,1280]{0,1:T(8,128)(2,1)S(1)} %convert.38, bf16[512,1280]{0,1:T(8,128)(2,1)S(1)} %multiply_convert_fusion), kind=kOutput, calls=%fused_computation.348 | convolution fusion | flops 3360686080 | bytes 17039360 | tf_op jit(solution)/shard_map/dot_general | solution.py:211
  180.6 7.0 %fusion.205 = f32[512,1280]{1,0:T(8,128)S(1)} fusion(bf16[1280,2560]{1,0:T(8,128)(2,1)} %all-gather.2.cloned.1.call-done, bf16[512,1280]{0,1:T(8,128)(2,1)} %copy-done.11, bf16[512,1280]{0,1:T(8,128)(2,1)S(1)} %multiply_convert_fusion), kind=kOutput, calls=%fused_computation.349 | convolution fusion | flops 3360686080 | bytes 11796480 | tf_op jit(solution)/shard_map/dot_general | solution.py:191
  187.7 6.7 %fusion.81 = (f32[1280]{0:T(1024)S(1)}, f32[1280]{0:T(1024)S(1)}, f32[1280]{0:T(1024)S(1)}, f32[1280]{0:T(1024)S(1)}, f32[1280]{0:T(1024)S(1)}, /*index=5*/f32[1...) fusion(bf16[1,527,1280]{2,1,0:T(8,128)(2,1)S(1)} %constant_dyna, ...), kind=kLoop, calls=%fused_computation.195 | loop fusion | flops 37335040 | bytes 27612160 | tf_op jit(solution)/shard_map/reduce_sum | solution.py:199
  194.6 2.6 fusion.52
  197.6 3.3 fusion.61
  202.3 4.6 collective-permute-start.11
  206.9 2.7 stack.127
  210.3 44.2 %psum.22 = f32[1280]{0:T(1024)} all-reduce(f32[1280]{0:T(1024)S(1)} %get-tuple-element.341), channel_id=1, replica_groups=mesh['dp'=16,'ctx'=2] {'dp','ctx'}, use_global_device_ids=true, to_apply=%region_39.40 | all-reduce | flops 1280 | bytes 10240 | tf_op jit(solution)/shard_map/psum | solution.py:209
  254.5 64.0 %reduce-scatter.2.cloned.1.call-done = f32[80,2560]{1,0:T(8,128)} async-done(((f32[1280,2560]{1,0:T(8,128)}), f32[80,2560]{1,0:T(8,128)}) %reduce-scatter.2.cloned.1.call-update) | async-done | bytes 819216 | tf_op jit(solution)/shard_map/reduce_scatter | solution.py:210
  318.8 43.9 %fusion.235 = bf16[1,512,1280]{2,1,0:T(8,128)(2,1)} fusion(f32[512,1280]{1,0:T(8,128)} %copy-done.6, f32[1,512,1280]{2,1,0:T(8,128)} %bitcast.634, f32[1,15,1280]{2,1,0:T(8,128)S(1)} %collective-permute-done.11, f32[1280]{0:T(1024)S(1)} %copy-done.33, f32[1280]{0:T(1024)S(1)} %copy-done.35, f32[1280]{0:T(1024)S(1)} %copy-done.39, f32[1280]{0:T(1024)S(1)} %copy-done.41, ...), kind=kLoop, calls=%fused_computation.396 | loop fusion | flops 60948480 | bytes 9487360 | tf_op jit(solution)/shard_map/broadcast_in_dim | solution.py:208
  362.7 83.9 %all-reduce.3.cloned.1.call-done = f32[31,1280]{1,0:T(8,128)} async-done(((f32[31,1280]{1,0:T(8,128)}), f32[31,1280]{1,0:T(8,128)}) %all-reduce.3.cloned.1.call-update) | async-done | bytes 158736 | tf_op jit(solution)/shard_map/psum | solution.py:209
  446.5 39.3 %all-reduce.5.cloned.1.call-done = f32[80,2560]{1,0:T(8,128)} async-done(((f32[80,2560]{1,0:T(8,128)}), f32[80,2560]{1,0:T(8,128)}) %all-reduce.5.cloned.1.call-update) | async-done | bytes 819216 | tf_op jit(solution)/shard_map/psum | solution.py:218
  (310 shorter events, 79.8 us)
Async XLA Ops:
  7.2 69.2 %all-gather.2.cloned.1.call-start = ((), (), s32[]{:S(2)}) async-start(), calls=%async_computation.1 | async-start | bytes 6963200 | tf_op jit(solution)/shard_map/all_gather | solution.py:114
  8.7 309.7 %reduce-scatter.2.cloned.1.call-start = ((), (), s32[]{:S(2)}) async-start(), calls=%async_computation.3 | async-start | bytes 13926400 | tf_op jit(solution)/shard_map/reduce_scatter | solution.py:210
  9.6 12.7 %collective-permute-start.8 = (bf16[1,15,1280]{2,1,0:T(8,128)(2,1)S(1)}, bf16[1,15,1280]{2,1,0:T(8,128)(2,1)S(1)}, u32[]{:S(2)}, u32[]{:S(2)}) collective-permute-start(bf16[1,15,1280]{2,1,0:T(8,128)(2,1)S(1)} %get-tuple-element.346), channel_id=1, source_target_pairs={{0,1},{2,3},{4,5},{6,7},{8,9},{10,11},{12,13},{14,15},{16,17},{18,... | collective-permute-start | bytes 115208 | tf_op jit(solution)/shard_map/ppermute | solution.py:14
  14.5 7.8 %collective-permute-start.9 = (bf16[1,15,1280]{2,1,0:T(8,128)(2,1)S(1)}, bf16[1,15,1280]{2,1,0:T(8,128)(2,1)S(1)}, u32[]{:S(2)}, u32[]{:S(2)}) collective-permute-start(bf16[1,15,1280]{2,1,0:T(8,128)(2,1)S(1)} %get-tuple-element.347), channel_id=1, source_target_pairs={{1,0},{3,2},{5,4},{7,6},{9,8},{11,10},{13,12},{15,14},{17,16},{19,... | collective-permute-start | bytes 115208 | tf_op jit(solution)/shard_map/ppermute | solution.py:17
  89.7 9.8 %collective-permute-start = (bf16[16,1280]{1,0:T(8,128)(2,1)S(1)}, bf16[16,1280]{1,0:T(8,128)(2,1)S(1)}, u32[]{:S(2)}, u32[]{:S(2)}) collective-permute-start(bf16[16,1280]{1,0:T(8,128)(2,1)S(1)} %copy.80), channel_id=1, source_target_pairs={{0,1},{1,0},{2,3},{3,2},{4,5},{5,4},{6,7},{7,6},{8,9},{9,8},{10,11... | collective-permute-start | bytes 122888 | tf_op jit(solution)/shard_map/while/body/eval_jaxpr/ppermute | solution.py:25
  94.3 5.1 %collective-permute-start.1 = (f32[16,1280]{1,0:T(8,128)S(1)}, f32[16,1280]{1,0:T(8,128)S(1)}, u32[]{:S(2)}, u32[]{:S(2)}) collective-permute-start(f32[16,1280]{1,0:T(8,128)S(1)} %add.1592), channel_id=1, source_target_pairs={{0,1},{1,0},{2,3},{3,2},{4,5},{5,4},{6,7},{7,6},{8,9},{9,8},{10,11... | collective-permute-start | bytes 245768 | tf_op jit(solution)/shard_map/while/body/eval_jaxpr/ppermute | solution.py:25
  95.7 3.8 collective-permute-start.2
  99.5 9.8 %collective-permute-start = (bf16[16,1280]{1,0:T(8,128)(2,1)S(1)}, bf16[16,1280]{1,0:T(8,128)(2,1)S(1)}, u32[]{:S(2)}, u32[]{:S(2)}) collective-permute-start(bf16[16,1280]{1,0:T(8,128)(2,1)S(1)} %copy.80), channel_id=1, source_target_pairs={{0,1},{1,0},{2,3},{3,2},{4,5},{5,4},{6,7},{7,6},{8,9},{9,8},{10,11... | collective-permute-start | bytes 122888 | tf_op jit(solution)/shard_map/while/body/eval_jaxpr/ppermute | solution.py:25
  104.1 5.1 %collective-permute-start.1 = (f32[16,1280]{1,0:T(8,128)S(1)}, f32[16,1280]{1,0:T(8,128)S(1)}, u32[]{:S(2)}, u32[]{:S(2)}) collective-permute-start(f32[16,1280]{1,0:T(8,128)S(1)} %add.1592), channel_id=1, source_target_pairs={{0,1},{1,0},{2,3},{3,2},{4,5},{5,4},{6,7},{7,6},{8,9},{9,8},{10,11... | collective-permute-start | bytes 245768 | tf_op jit(solution)/shard_map/while/body/eval_jaxpr/ppermute | solution.py:25
  105.5 3.8 collective-permute-start.2
  113.8 25.9 %collective-permute-start.5 = (f32[16,20]{0,1:T(8,128)}, f32[16,20]{0,1:T(8,128)}, u32[]{:S(2)}, u32[]{:S(2)}) collective-permute-start(f32[16,20]{0,1:T(8,128)} %copy.98), channel_id=1, source_target_pairs={{0,1},{1,0},{2,3},{3,2},{4,5},{5,4},{6,7},{7,6},{8,9},{9,8},{10,11... | collective-permute-start | bytes 3848 | tf_op jit(solution)/shard_map/while/body/eval_jaxpr/ppermute | solution.py:25
  116.6 23.1 %collective-permute-start.6 = (f32[16,20]{0,1:T(8,128)}, f32[16,20]{0,1:T(8,128)}, u32[]{:S(2)}, u32[]{:S(2)}) collective-permute-start(f32[16,20]{0,1:T(8,128)} %copy.99), channel_id=1, source_target_pairs={{0,1},{1,0},{2,3},{3,2},{4,5},{5,4},{6,7},{7,6},{8,9},{9,8},{10,11... | collective-permute-start | bytes 3848 | tf_op jit(solution)/shard_map/while/body/eval_jaxpr/ppermute | solution.py:25
  117.9 21.8 %collective-permute-start.3 = (bf16[16,1280]{1,0:T(8,128)(2,1)S(1)}, bf16[16,1280]{1,0:T(8,128)(2,1)}, u32[]{:S(2)}, u32[]{:S(2)}) collective-permute-start(bf16[16,1280]{1,0:T(8,128)(2,1)S(1)} %copy.96), channel_id=1, source_target_pairs={{0,1},{1,0},{2,3},{3,2},{4,5},{5,4},{6,7},{7,6},{8,9},{9,8},{10,11... | collective-permute-start | bytes 122888 | tf_op jit(solution)/shard_map/while/body/eval_jaxpr/ppermute | solution.py:25
  120.2 19.5 %collective-permute-start.4 = (bf16[16,1280]{1,0:T(8,128)(2,1)S(1)}, bf16[16,1280]{1,0:T(8,128)(2,1)}, u32[]{:S(2)}, u32[]{:S(2)}) collective-permute-start(bf16[16,1280]{1,0:T(8,128)(2,1)S(1)} %copy.97), channel_id=1, source_target_pairs={{0,1},{1,0},{2,3},{3,2},{4,5},{5,4},{6,7},{7,6},{8,9},{9,8},{10,11... | collective-permute-start | bytes 122888 | tf_op jit(solution)/shard_map/while/body/eval_jaxpr/ppermute | solution.py:25
  126.7 13.0 %collective-permute-start.7 = (f32[16,1280]{1,0:T(8,128)S(1)}, f32[16,1280]{1,0:T(8,128)S(1)}, u32[]{:S(2)}, u32[]{:S(2)}) collective-permute-start(f32[16,1280]{1,0:T(8,128)S(1)} %add.1597), channel_id=1, source_target_pairs={{0,1},{1,0},{2,3},{3,2},{4,5},{5,4},{6,7},{7,6},{8,9},{9,8},{10,11... | collective-permute-start | bytes 245768 | tf_op jit(solution)/shard_map/while/body/eval_jaxpr/ppermute | solution.py:25
  141.7 26.5 %collective-permute-start.5 = (f32[16,20]{0,1:T(8,128)}, f32[16,20]{0,1:T(8,128)}, u32[]{:S(2)}, u32[]{:S(2)}) collective-permute-start(f32[16,20]{0,1:T(8,128)} %copy.98), channel_id=1, source_target_pairs={{0,1},{1,0},{2,3},{3,2},{4,5},{5,4},{6,7},{7,6},{8,9},{9,8},{10,11... | collective-permute-start | bytes 3848 | tf_op jit(solution)/shard_map/while/body/eval_jaxpr/ppermute | solution.py:25
  143.5 24.6 %collective-permute-start.6 = (f32[16,20]{0,1:T(8,128)}, f32[16,20]{0,1:T(8,128)}, u32[]{:S(2)}, u32[]{:S(2)}) collective-permute-start(f32[16,20]{0,1:T(8,128)} %copy.99), channel_id=1, source_target_pairs={{0,1},{1,0},{2,3},{3,2},{4,5},{5,4},{6,7},{7,6},{8,9},{9,8},{10,11... | collective-permute-start | bytes 3848 | tf_op jit(solution)/shard_map/while/body/eval_jaxpr/ppermute | solution.py:25
  145.8 22.4 %collective-permute-start.3 = (bf16[16,1280]{1,0:T(8,128)(2,1)S(1)}, bf16[16,1280]{1,0:T(8,128)(2,1)}, u32[]{:S(2)}, u32[]{:S(2)}) collective-permute-start(bf16[16,1280]{1,0:T(8,128)(2,1)S(1)} %copy.96), channel_id=1, source_target_pairs={{0,1},{1,0},{2,3},{3,2},{4,5},{5,4},{6,7},{7,6},{8,9},{9,8},{10,11... | collective-permute-start | bytes 122888 | tf_op jit(solution)/shard_map/while/body/eval_jaxpr/ppermute | solution.py:25
  147.1 21.1 %collective-permute-start.4 = (bf16[16,1280]{1,0:T(8,128)(2,1)S(1)}, bf16[16,1280]{1,0:T(8,128)(2,1)}, u32[]{:S(2)}, u32[]{:S(2)}) collective-permute-start(bf16[16,1280]{1,0:T(8,128)(2,1)S(1)} %copy.97), channel_id=1, source_target_pairs={{0,1},{1,0},{2,3},{3,2},{4,5},{5,4},{6,7},{7,6},{8,9},{9,8},{10,11... | collective-permute-start | bytes 122888 | tf_op jit(solution)/shard_map/while/body/eval_jaxpr/ppermute | solution.py:25
  154.6 13.6 %collective-permute-start.7 = (f32[16,1280]{1,0:T(8,128)S(1)}, f32[16,1280]{1,0:T(8,128)S(1)}, u32[]{:S(2)}, u32[]{:S(2)}) collective-permute-start(f32[16,1280]{1,0:T(8,128)S(1)} %add.1597), channel_id=1, source_target_pairs={{0,1},{1,0},{2,3},{3,2},{4,5},{5,4},{6,7},{7,6},{8,9},{9,8},{10,11... | collective-permute-start | bytes 245768 | tf_op jit(solution)/shard_map/while/body/eval_jaxpr/ppermute | solution.py:25
  180.4 266.2 %all-reduce.3.cloned.1.call-start = ((), (), s32[]{:S(2)}) async-start(), calls=%async_computation.2 | async-start | bytes 327680 | tf_op jit(solution)/shard_map/psum | solution.py:209
  201.0 117.5 %collective-permute-start.10 = (f32[1,15,1280]{2,1,0:T(8,128)S(1)}, f32[1,15,1280]{2,1,0:T(8,128)S(1)}, u32[]{:S(2)}, u32[]{:S(2)}) collective-permute-start(f32[1,15,1280]{2,1,0:T(8,128)S(1)} %get-tuple-element.342), channel_id=1, source_target_pairs={{1,0},{3,2},{5,4},{7,6},{9,8},{11,10},{13,12},{15,14},{17,16},{19,... | collective-permute-start | bytes 230408 | tf_op jit(solution)/shard_map/ppermute | solution.py:17
  202.3 116.2 %collective-permute-start.11 = (f32[1,15,1280]{2,1,0:T(8,128)S(1)}, f32[1,15,1280]{2,1,0:T(8,128)S(1)}, u32[]{:S(2)}, u32[]{:S(2)}) collective-permute-start(f32[1,15,1280]{2,1,0:T(8,128)S(1)} %get-tuple-element.343), channel_id=1, source_target_pairs={{0,1},{2,3},{4,5},{6,7},{8,9},{10,11},{12,13},{14,15},{16,17},{18,... | collective-permute-start | bytes 230408 | tf_op jit(solution)/shard_map/ppermute | solution.py:14
  209.6 276.3 %all-reduce.5.cloned.1.call-start = ((), (), s32[]{:S(2)}) async-start(), calls=%async_computation.4 | async-start | bytes 1638400 | tf_op jit(solution)/shard_map/psum | solution.py:218
  (80 other events, 4241.4 us)
Sparse Core Ops, SparseCore 0:
  10.3 66.0 all-gather.1
  180.5 137.9 reduce-scatter.1
  325.5 120.9 all-reduce.2
  448.8 37.0 all-reduce.4
where the time goes:
time: 498 us; the launch traced here: 496 us
  waiting for transfers between devices  233 us (47%)
  other arithmetic  92.3 us (19%)
  blocking collectives  44.2 us (9%)
  matrix products  42.7 us (9%)
  local copies, waits for them, and re-layouts  37.5 us (8%)
  starting transfers between devices  29.8 us (6%)
  between operations  16 us (3%)
    psum x1, waiting for transfers between devices, per_device(): taps_grad, gain_grad = lax.psum((tap_terms, gain_term), ('dp', 'ctx'))  83.9 us
    reduce_scatter x1, waiting for transfers between devices, per_device(): lax.psum_scatter(lax.dot_general(encoded, kv_grad, (((0,), (0,)), ((), ()...  64 us
    psum x1, blocking collectives, per_device(): taps_grad, gain_grad = lax.psum((tap_terms, gain_term), ('dp', 'ctx'))  44.2 us
    broadcast_in_dim x1, other arithmetic, per_device(): frames_grad = (enc_grad + back_conv).astype(jnp.bfloat16)[None]  43.9 us
    all_gather x1, waiting for transfers between devices, per_device(): w_full = lax.all_gather(w_kv, 'dp', axis=0, tiled=True)  41.4 us
    psum x1, waiting for transfers between devices, per_device(): w_kv_grad = lax.psum(data_part, 'ctx')  39.3 us
    ppermute x16, starting transfers between devices, shifted(): return lax.ppermute(value, axis, pairs)  17.5 us
    unnamed x156, local copies, waits for them, and re-layouts  13.9 us
  transfers between devices with their start and end apart: 24, of which 6 were waited for; matrix products, arithmetic and copies ran while one was open for 27% of the time, Pallas kernels for 0%

commit v1 on v0

--- a/solution.py
+++ b/solution.py
@@ -111,7 +111,12 @@
     conv_out = conv_time(padded, conv_taps, length)
     gated = conv_gain * conv_out
     encoded = (frames[0].astype(jnp.float32) + jax.nn.silu(gated)).astype(jnp.bfloat16)
-    w_full = lax.all_gather(w_kv, "dp", axis=0, tiled=True)
+    ring = [w_kv]
+    for hop in range(15):
+        ring.append(lax.ppermute(ring[-1], "dp", [(dev, (dev + 1) % 16) for dev in range(16)]))
+    w_full = jnp.roll(
+        jnp.concatenate(ring[::-1], axis=0), (lax.axis_index("dp") + 1) * ring[0].shape[0], axis=0
+    )
     key_values = jnp.dot(encoded, w_full, preferred_element_type=jnp.float32).astype(jnp.bfloat16)
     key_block = key_values[:, :model_width]
     value_block = key_values[:, model_width:]

time: 498 us -> 551 us (1.11)
  waiting for transfers between devices: 233 us -> 266 us
  local copies, waits for them, and re-layouts: 37.5 us -> 53.8 us
    ppermute x0 -> x15, waiting for transfers between devices: none -> 126 us  [per_device(): lax.ppermute(ring[-1], 'dp', [(dev, (dev + 1) % 16) for dev in range(16)])]
    psum x1, waiting for transfers between devices: 83.9 us -> 34.8 us  [per_device(): taps_grad, gain_grad = lax.psum((tap_terms, gain_term), ('dp', 'ctx'))]
    all_gather x1 -> x0, waiting for transfers between devices: 41.4 us -> none  [per_device(): w_full = lax.all_gather(w_kv, 'dp', axis=0, tiled=True)]
    unnamed x156 -> x167, local copies, waits for them, and re-layouts: 13.9 us -> 27.9 us
  transfers between devices with their start and end apart: 24 -> 38, of which waited for: 6 -> 19; matrix products, arithmetic and copies ran while one was open for 27% -> 26% of each run, Pallas kernels for 0% -> 0%
where the time goes in v1:
time: 551 us; the launch traced here: 548 us
  waiting for transfers between devices  266 us (48%)
  other arithmetic  97.4 us (18%)
  local copies, waits for them, and re-layouts  53.8 us (10%)
  blocking collectives  43 us (8%)
  matrix products  39.9 us (7%)
  starting transfers between devices  30.8 us (6%)
  between operations  17.6 us (3%)
    ppermute x15, waiting for transfers between devices, per_device(): lax.ppermute(ring[-1], 'dp', [(dev, (dev + 1) % 16) for dev in range(16)])  126 us
    reduce_scatter x1, waiting for transfers between devices, per_device(): lax.psum_scatter(lax.dot_general(encoded, kv_grad, (((0,), (0,)), ((), ()...  62.1 us
    psum x1, blocking collectives, per_device(): taps_grad, gain_grad = lax.psum((tap_terms, gain_term), ('dp', 'ctx'))  43 us
    broadcast_in_dim x1, other arithmetic, per_device(): frames_grad = (enc_grad + back_conv).astype(jnp.bfloat16)[None]  42.1 us
    psum x1, waiting for transfers between devices, per_device(): w_kv_grad = lax.psum(data_part, 'ctx')  39.1 us
    psum x1, waiting for transfers between devices, per_device(): taps_grad, gain_grad = lax.psum((tap_terms, gain_term), ('dp', 'ctx'))  34.8 us
    unnamed x167, local copies, waits for them, and re-layouts  27.9 us
    ppermute x16, starting transfers between devices, shifted(): return lax.ppermute(value, axis, pairs)  18.4 us
  transfers between devices with their start and end apart: 38, of which 19 were waited for; matrix products, arithmetic and copies ran while one was open for 26% of the time, Pallas kernels for 0%

profile of v1, /device:TPU:0, one launch (start us, length us, event | category | flops | bytes accessed | tf_op | source)
XLA Modules:
  0.0 548.4 jit_solution(4749381783520045851)
XLA Ops:
  10.0 10.8 %collective-permute-done.10 = bf16[80,2560]{1,0:T(8,128)(2,1)S(1)} collective-permute-done((bf16[80,2560]{1,0:T(8,128)(2,1)}, bf16[80,2560]{1,0:T(8,128)(2,1)S(1)}, u32[]{:S(2)}, u32[]{:S(2)}) %collective-permute-start.10) | collective-permute-done | bytes 409632 | tf_op jit(solution)/shard_map/ppermute | solution.py:116
  20.8 10.1 %collective-permute-done.11 = bf16[80,2560]{1,0:T(8,128)(2,1)S(1)} collective-permute-done((bf16[80,2560]{1,0:T(8,128)(2,1)S(1)}, bf16[80,2560]{1,0:T(8,128)(2,1)S(1)}, u32[]{:S(2)}, u32[]{:S(2)}) %collective-permute-start.11) | collective-permute-done | bytes 409632 | tf_op jit(solution)/shard_map/ppermute | solution.py:116
  30.9 10.1 %collective-permute-done.12 = bf16[80,2560]{1,0:T(8,128)(2,1)S(1)} collective-permute-done((bf16[80,2560]{1,0:T(8,128)(2,1)S(1)}, bf16[80,2560]{1,0:T(8,128)(2,1)S(1)}, u32[]{:S(2)}, u32[]{:S(2)}) %collective-permute-start.12) | collective-permute-done | bytes 409632 | tf_op jit(solution)/shard_map/ppermute | solution.py:116
  41.0 10.1 %collective-permute-done.13 = bf16[80,2560]{1,0:T(8,128)(2,1)S(1)} collective-permute-done((bf16[80,2560]{1,0:T(8,128)(2,1)S(1)}, bf16[80,2560]{1,0:T(8,128)(2,1)S(1)}, u32[]{:S(2)}, u32[]{:S(2)}) %collective-permute-start.13) | collective-permute-done | bytes 409632 | tf_op jit(solution)/shard_map/ppermute | solution.py:116
  51.1 10.1 %collective-permute-done.14 = bf16[80,2560]{1,0:T(8,128)(2,1)S(1)} collective-permute-done((bf16[80,2560]{1,0:T(8,128)(2,1)S(1)}, bf16[80,2560]{1,0:T(8,128)(2,1)S(1)}, u32[]{:S(2)}, u32[]{:S(2)}) %collective-permute-start.14) | collective-permute-done | bytes 409632 | tf_op jit(solution)/shard_map/ppermute | solution.py:116
  61.1 10.1 %collective-permute-done.15 = bf16[80,2560]{1,0:T(8,128)(2,1)S(1)} collective-permute-done((bf16[80,2560]{1,0:T(8,128)(2,1)S(1)}, bf16[80,2560]{1,0:T(8,128)(2,1)S(1)}, u32[]{:S(2)}, u32[]{:S(2)}) %collective-permute-start.15) | collective-permute-done | bytes 409632 | tf_op jit(solution)/shard_map/ppermute | solution.py:116
  72.0 10.1 %collective-permute-done.16 = bf16[80,2560]{1,0:T(8,128)(2,1)S(1)} collective-permute-done((bf16[80,2560]{1,0:T(8,128)(2,1)S(1)}, bf16[80,2560]{1,0:T(8,128)(2,1)S(1)}, u32[]{:S(2)}, u32[]{:S(2)}) %collective-permute-start.16) | collective-permute-done | bytes 409632 | tf_op jit(solution)/shard_map/ppermute | solution.py:116
  82.8 10.1 %collective-permute-done.17 = bf16[80,2560]{1,0:T(8,128)(2,1)S(1)} collective-permute-done((bf16[80,2560]{1,0:T(8,128)(2,1)S(1)}, bf16[80,2560]{1,0:T(8,128)(2,1)S(1)}, u32[]{:S(2)}, u32[]{:S(2)}) %collective-permute-start.17) | collective-permute-done | bytes 409632 | tf_op jit(solution)/shard_map/ppermute | solution.py:116
  93.6 10.1 %collective-permute-done.18 = bf16[80,2560]{1,0:T(8,128)(2,1)S(1)} collective-permute-done((bf16[80,2560]{1,0:T(8,128)(2,1)S(1)}, bf16[80,2560]{1,0:T(8,128)(2,1)S(1)}, u32[]{:S(2)}, u32[]{:S(2)}) %collective-permute-start.18) | collective-permute-done | bytes 409632 | tf_op jit(solution)/shard_map/ppermute | solution.py:116
  104.4 10.1 %collective-permute-done.19 = bf16[80,2560]{1,0:T(8,128)(2,1)S(1)} collective-permute-done((bf16[80,2560]{1,0:T(8,128)(2,1)S(1)}, bf16[80,2560]{1,0:T(8,128)(2,1)S(1)}, u32[]{:S(2)}, u32[]{:S(2)}) %collective-permute-start.19) | collective-permute-done | bytes 409632 | tf_op jit(solution)/shard_map/ppermute | solution.py:116
  115.3 10.2 %collective-permute-done.20 = bf16[80,2560]{1,0:T(8,128)(2,1)} collective-permute-done((bf16[80,2560]{1,0:T(8,128)(2,1)S(1)}, bf16[80,2560]{1,0:T(8,128)(2,1)}, u32[]{:S(2)}, u32[]{:S(2)}) %collective-permute-start.20) | collective-permute-done | bytes 409632 | tf_op jit(solution)/shard_map/ppermute | solution.py:116
  139.7 6.5 %collective-permute-done.22 = bf16[80,2560]{1,0:T(8,128)(2,1)} collective-permute-done((bf16[80,2560]{1,0:T(8,128)(2,1)}, bf16[80,2560]{1,0:T(8,128)(2,1)}, u32[]{:S(2)}, u32[]{:S(2)}) %collective-permute-start.22) | collective-permute-done | bytes 409632 | tf_op jit(solution)/shard_map/ppermute | solution.py:116
  156.6 15.2 %fusion.89 = (bf16[512,1280]{1,0:T(8,128)(2,1)S(1)}, f32[512,1280]{1,0:T(8,128)}) fusion(bf16[1,512,1280]{2,1,0:T(8,128)(2,1)S(1)} %copy-done.4, f32[1280]{0:T(1024)} %param.14, bf16[1,527,1280]{2,1,0:T(8,128)(2,1)S(1)} %constant_dynamic-update-slice_fusion, f32[1280]{0:T(1024)} %get-tuple-element.290, f32[1280]{0:T(1024)} %get-tuple-element.291, ...), kind=kLoop, calls=%fused_computation.200 | loop fusion | flops 104202240 | bytes 25105920 | tf_op jit(solution)/shard_map/convert_element_type | solution.py:113
  192.4 19.8 %while.38 = (s32[]{:T(128)}, bf16[16,1280]{1,0:T(8,128)(2,1)S(1)}, f32[16,1280]{1,0:T(8,128)S(1)}, f32[16,20]{0,1:T(8,128)}, bf16[512,1280]{0,1:T(8,128)(2,1)}, ...) while((s32[]{:T(128)}, bf16[16,1280]{1,0:T(8,128)(2,1)S(1)}, ...), condition=%wide.region_2.3_spmd.clone, body=%wide.region_0.2_spmd.clone.sunk | while | flops 42620416 | bytes 4643037 | solution.py:158
  215.4 56.2 %while.39 = (s32[]{:T(128)}, bf16[16,1280]{1,0:T(8,128)(2,1)}, bf16[16,1280]{1,0:T(8,128)(2,1)}, f32[16,20]{0,1:T(8,128)}, f32[16,20]{0,1:T(8,128)}, /*index=5*/...) while((s32[]{:T(128)}, bf16[16,1280]{1,0:T(8,128)(2,1)}, ...), condition=%wide.region_5.6_spmd.clone, body=%wide.region_4.5_spmd.clone.sunk | while | flops 108647936 | bytes 37869488 | solution.py:190
  263.3 7.7 %bitcast_add_fusion.6 = (f32[512,1280]{0,1:T(8,128)}, f32[512,1280]{0,1:T(8,128)}) fusion(f32[20,512,64]{1,2,0:T(8,128)} %fusion.300, f32[512,1280]{0,1:T(8,128)} %get-tuple-element.528, pred[]{:T(512)S(6)} %compare.3, f32[20,512,64]{1,2,0:T(8,128)} %fusion.301, f32[512,1280]{0,1:T(8,128)} %get-tuple-element.527), kind=kLoop, calls=%fused_computation.11.clone.1 | loop fusion | flops 2621440 | bytes 15728641 | tf_op jit(solution)/shard_map/while/body/eval_jaxpr/add | solution.py:178
  275.6 7.6 %fusion.211 = f32[1280,2560]{1,0:T(8,128)} fusion(bf16[512,1280]{1,0:T(8,128)(2,1)S(1)} %copy-done.28, bf16[512,1280]{0,1:T(8,128)(2,1)S(1)} %convert.38, bf16[512,1280]{0,1:T(8,128)(2,1)S(1)} %multiply_convert_fusion), kind=kOutput, calls=%fused_computation.352 | convolution fusion | flops 3360686080 | bytes 17039360 | tf_op jit(solution)/shard_map/dot_general | solution.py:216
  283.3 7.4 %fusion.22 = f32[512,1280]{1,0:T(8,128)S(1)} fusion(bf16[2560,2560]{1,0:T(8,128)(2,1)} %copy-done.65, s32[]{:T(128)S(6)} %select_n.14, bf16[512,1280]{0,1:T(8,128)(2,1)S(1)} %convert.38, bf16[512,1280]{0,1:T(8,128)(2,1)} %copy-done.29), kind=kOutput, calls=%fused_computation.72 | convolution fusion | flops 3360686080 | bytes 11796484 | tf_op jit(solution)/shard_map/dot_general | solution.py:196
  290.8 6.7 %fusion.88 = (f32[1280]{0:T(1024)S(1)}, f32[1280]{0:T(1024)S(1)}, f32[1280]{0:T(1024)S(1)}, f32[1280]{0:T(1024)S(1)}, f32[1280]{0:T(1024)S(1)}, /*index=5*/f32[1...) fusion(bf16[1,527,1280]{2,1,0:T(8,128)(2,1)S(1)} %constant_dyna, ...), kind=kLoop, calls=%fused_computation.199 | loop fusion | flops 37335040 | bytes 27612160 | tf_op jit(solution)/shard_map/reduce_sum | solution.py:204
  315.8 43.0 %psum.22 = f32[1280]{0:T(1024)} all-reduce(f32[1280]{0:T(1024)S(1)} %get-tuple-element.341), channel_id=1, replica_groups=mesh['dp'=16,'ctx'=2] {'dp','ctx'}, use_global_device_ids=true, to_apply=%region_39.40 | all-reduce | flops 1280 | bytes 10240 | tf_op jit(solution)/shard_map/psum | solution.py:214
  358.8 62.1 %reduce-scatter.2.cloned.1.call-done = f32[80,2560]{1,0:T(8,128)} async-done(((f32[1280,2560]{1,0:T(8,128)}), f32[80,2560]{1,0:T(8,128)}) %reduce-scatter.2.cloned.1.call-update) | async-done | bytes 819216 | tf_op jit(solution)/shard_map/reduce_scatter | solution.py:215
  421.2 42.1 %fusion.241 = bf16[1,512,1280]{2,1,0:T(8,128)(2,1)} fusion(f32[512,1280]{1,0:T(8,128)} %copy-done.6, f32[1,512,1280]{2,1,0:T(8,128)} %bitcast.632, f32[1,15,1280]{2,1,0:T(8,128)S(1)} %collective-permute-done.26, f32[1280]{0:T(1024)S(1)} %copy-done.61, f32[1280]{0:T(1024)S(1)} %copy-done.62, f32[1280]{0:T(1024)S(1)} %copy-done.31, f32[1280]{0:T(1024)S(1)} %copy-done.33, ...), kind=kLoop, calls=%fused_computation.399 | loop fusion | flops 60948480 | bytes 9487360 | tf_op jit(solution)/shard_map/broadcast_in_dim | solution.py:213
  463.4 34.8 %all-reduce.3.cloned.1.call-done = f32[31,1280]{1,0:T(8,128)} async-done(((f32[31,1280]{1,0:T(8,128)}), f32[31,1280]{1,0:T(8,128)}) %all-reduce.3.cloned.1.call-update) | async-done | bytes 158736 | tf_op jit(solution)/shard_map/psum | solution.py:214
  498.1 39.1 %all-reduce.5.cloned.1.call-done = f32[80,2560]{1,0:T(8,128)} async-done(((f32[80,2560]{1,0:T(8,128)}), f32[80,2560]{1,0:T(8,128)}) %all-reduce.5.cloned.1.call-update) | async-done | bytes 819216 | tf_op jit(solution)/shard_map/psum | solution.py:223
  (349 shorter events, 146.6 us)
Async XLA Ops:
  8.0 412.9 %reduce-scatter.2.cloned.1.call-start = ((), (), s32[]{:S(2)}) async-start(), calls=%async_computation.2 | async-start | bytes 13926400 | tf_op jit(solution)/shard_map/reduce_scatter | solution.py:215
  9.5 11.3 %collective-permute-start.10 = (bf16[80,2560]{1,0:T(8,128)(2,1)}, bf16[80,2560]{1,0:T(8,128)(2,1)S(1)}, u32[]{:S(2)}, u32[]{:S(2)}) collective-permute-start(bf16[80,2560]{1,0:T(8,128)(2,1)} %param.15), channel_id=1, source_target_pairs={{0,2},{2,4},{4,6},{6,8},{8,10},{10,12},{12,14},{14,16},{16,18},{18... | collective-permute-start | bytes 1228808 | tf_op jit(solution)/shard_map/ppermute | solution.py:116
  72.0 10.1 %collective-permute-start.16 = (bf16[80,2560]{1,0:T(8,128)(2,1)S(1)}, bf16[80,2560]{1,0:T(8,128)(2,1)S(1)}, u32[]{:S(2)}, u32[]{:S(2)}) collective-permute-start(bf16[80,2560]{1,0:T(8,128)(2,1)S(1)} %collective-permute-done.15), channel_id=1, source_target_pairs={{0,2},{2,4},{4,6},{6,8},{8,10},{10,12},{12,14},{14,16},{16,18},{18... | collective-permute-start | bytes 1228808 | tf_op jit(solution)/shard_map/ppermute | solution.py:116
  115.3 10.2 %collective-permute-start.20 = (bf16[80,2560]{1,0:T(8,128)(2,1)S(1)}, bf16[80,2560]{1,0:T(8,128)(2,1)}, u32[]{:S(2)}, u32[]{:S(2)}) collective-permute-start(bf16[80,2560]{1,0:T(8,128)(2,1)S(1)} %collective-permute-done.19), channel_id=1, source_target_pairs={{0,2},{2,4},{4,6},{6,8},{8,10},{10,12},{12,14},{14,16},{16,18},{18... | collective-permute-start | bytes 1228808 | tf_op jit(solution)/shard_map/ppermute | solution.py:116
  125.4 10.4 %collective-permute-start.21 = (bf16[80,2560]{1,0:T(8,128)(2,1)}, bf16[80,2560]{1,0:T(8,128)(2,1)}, u32[]{:S(2)}, u32[]{:S(2)}) collective-permute-start(bf16[80,2560]{1,0:T(8,128)(2,1)} %collective-permute-done.20), channel_id=1, source_target_pairs={{0,2},{2,4},{4,6},{6,8},{8,10},{10,12},{12,14},{14,16},{16,18},{18... | collective-permute-start | bytes 1228808 | tf_op jit(solution)/shard_map/ppermute | solution.py:116
  126.9 22.8 %collective-permute-start.9 = (bf16[1,15,1280]{2,1,0:T(8,128)(2,1)}, bf16[1,15,1280]{2,1,0:T(8,128)(2,1)}, u32[]{:S(2)}, u32[]{:S(2)}) collective-permute-start(bf16[1,15,1280]{2,1,0:T(8,128)(2,1)} %get-tuple-element.347), channel_id=1, source_target_pairs={{1,0},{3,2},{5,4},{7,6},{9,8},{11,10},{13,12},{15,14},{17,16},{19,... | collective-permute-start | bytes 115208 | tf_op jit(solution)/shard_map/ppermute | solution.py:17
  128.2 28.4 %collective-permute-start.8 = (bf16[1,15,1280]{2,1,0:T(8,128)(2,1)}, bf16[1,15,1280]{2,1,0:T(8,128)(2,1)}, u32[]{:S(2)}, u32[]{:S(2)}) collective-permute-start(bf16[1,15,1280]{2,1,0:T(8,128)(2,1)} %get-tuple-element.346), channel_id=1, source_target_pairs={{0,1},{2,3},{4,5},{6,7},{8,9},{10,11},{12,13},{14,15},{16,17},{18,... | collective-permute-start | bytes 115208 | tf_op jit(solution)/shard_map/ppermute | solution.py:14
  135.8 10.4 %collective-permute-start.22 = (bf16[80,2560]{1,0:T(8,128)(2,1)}, bf16[80,2560]{1,0:T(8,128)(2,1)}, u32[]{:S(2)}, u32[]{:S(2)}) collective-permute-start(bf16[80,2560]{1,0:T(8,128)(2,1)} %collective-permute-done.21), channel_id=1, source_target_pairs={{0,2},{2,4},{4,6},{6,8},{8,10},{10,12},{12,14},{14,16},{16,18},{18... | collective-permute-start | bytes 1228808 | tf_op jit(solution)/shard_map/ppermute | solution.py:116
  146.2 10.4 %collective-permute-start.23 = (bf16[80,2560]{1,0:T(8,128)(2,1)}, bf16[80,2560]{1,0:T(8,128)(2,1)}, u32[]{:S(2)}, u32[]{:S(2)}) collective-permute-start(bf16[80,2560]{1,0:T(8,128)(2,1)} %collective-permute-done.22), channel_id=1, source_target_pairs={{0,2},{2,4},{4,6},{6,8},{8,10},{10,12},{12,14},{14,16},{16,18},{18... | collective-permute-start | bytes 1228808 | tf_op jit(solution)/shard_map/ppermute | solution.py:116
  156.6 15.3 %collective-permute-start.24 = (bf16[80,2560]{1,0:T(8,128)(2,1)}, bf16[80,2560]{1,0:T(8,128)(2,1)S(1)}, u32[]{:S(2)}, u32[]{:S(2)}) collective-permute-start(bf16[80,2560]{1,0:T(8,128)(2,1)} %collective-permute-done.23), channel_id=1, source_target_pairs={{0,2},{2,4},{4,6},{6,8},{8,10},{10,12},{12,14},{14,16},{16,18},{18... | collective-permute-start | bytes 1228808 | tf_op jit(solution)/shard_map/ppermute | solution.py:116
  216.2 26.6 %collective-permute-start.3 = (bf16[16,1280]{1,0:T(8,128)(2,1)S(1)}, bf16[16,1280]{1,0:T(8,128)(2,1)}, u32[]{:S(2)}, u32[]{:S(2)}) collective-permute-start(bf16[16,1280]{1,0:T(8,128)(2,1)S(1)} %copy.127), channel_id=1, source_target_pairs={{0,1},{1,0},{2,3},{3,2},{4,5},{5,4},{6,7},{7,6},{8,9},{9,8},{10,11... | collective-permute-start | bytes 122888 | tf_op jit(solution)/shard_map/while/body/eval_jaxpr/ppermute | solution.py:25
  218.7 24.1 %collective-permute-start.4 = (bf16[16,1280]{1,0:T(8,128)(2,1)S(1)}, bf16[16,1280]{1,0:T(8,128)(2,1)}, u32[]{:S(2)}, u32[]{:S(2)}) collective-permute-start(bf16[16,1280]{1,0:T(8,128)(2,1)S(1)} %copy.128), channel_id=1, source_target_pairs={{0,1},{1,0},{2,3},{3,2},{4,5},{5,4},{6,7},{7,6},{8,9},{9,8},{10,11... | collective-permute-start | bytes 122888 | tf_op jit(solution)/shard_map/while/body/eval_jaxpr/ppermute | solution.py:25
  220.3 22.5 %collective-permute-start.5 = (f32[16,20]{0,1:T(8,128)}, f32[16,20]{0,1:T(8,128)}, u32[]{:S(2)}, u32[]{:S(2)}) collective-permute-start(f32[16,20]{0,1:T(8,128)} %copy.129), channel_id=1, source_target_pairs={{0,1},{1,0},{2,3},{3,2},{4,5},{5,4},{6,7},{7,6},{8,9},{9,8},{10,11... | collective-permute-start | bytes 3848 | tf_op jit(solution)/shard_map/while/body/eval_jaxpr/ppermute | solution.py:25
  223.4 19.5 %collective-permute-start.6 = (f32[16,20]{0,1:T(8,128)}, f32[16,20]{0,1:T(8,128)}, u32[]{:S(2)}, u32[]{:S(2)}) collective-permute-start(f32[16,20]{0,1:T(8,128)} %copy.130), channel_id=1, source_target_pairs={{0,1},{1,0},{2,3},{3,2},{4,5},{5,4},{6,7},{7,6},{8,9},{9,8},{10,11... | collective-permute-start | bytes 3848 | tf_op jit(solution)/shard_map/while/body/eval_jaxpr/ppermute | solution.py:25
  229.7 13.2 %collective-permute-start.7 = (f32[16,1280]{1,0:T(8,128)S(1)}, f32[16,1280]{1,0:T(8,128)S(1)}, u32[]{:S(2)}, u32[]{:S(2)}) collective-permute-start(f32[16,1280]{1,0:T(8,128)S(1)} %add.1613), channel_id=1, source_target_pairs={{0,1},{1,0},{2,3},{3,2},{4,5},{5,4},{6,7},{7,6},{8,9},{9,8},{10,11... | collective-permute-start | bytes 245768 | tf_op jit(solution)/shard_map/while/body/eval_jaxpr/ppermute | solution.py:25
  244.3 26.7 %collective-permute-start.3 = (bf16[16,1280]{1,0:T(8,128)(2,1)S(1)}, bf16[16,1280]{1,0:T(8,128)(2,1)}, u32[]{:S(2)}, u32[]{:S(2)}) collective-permute-start(bf16[16,1280]{1,0:T(8,128)(2,1)S(1)} %copy.127), channel_id=1, source_target_pairs={{0,1},{1,0},{2,3},{3,2},{4,5},{5,4},{6,7},{7,6},{8,9},{9,8},{10,11... | collective-permute-start | bytes 122888 | tf_op jit(solution)/shard_map/while/body/eval_jaxpr/ppermute | solution.py:25
  245.4 25.6 %collective-permute-start.4 = (bf16[16,1280]{1,0:T(8,128)(2,1)S(1)}, bf16[16,1280]{1,0:T(8,128)(2,1)}, u32[]{:S(2)}, u32[]{:S(2)}) collective-permute-start(bf16[16,1280]{1,0:T(8,128)(2,1)S(1)} %copy.128), channel_id=1, source_target_pairs={{0,1},{1,0},{2,3},{3,2},{4,5},{5,4},{6,7},{7,6},{8,9},{9,8},{10,11... | collective-permute-start | bytes 122888 | tf_op jit(solution)/shard_map/while/body/eval_jaxpr/ppermute | solution.py:25
  248.4 22.6 %collective-permute-start.5 = (f32[16,20]{0,1:T(8,128)}, f32[16,20]{0,1:T(8,128)}, u32[]{:S(2)}, u32[]{:S(2)}) collective-permute-start(f32[16,20]{0,1:T(8,128)} %copy.129), channel_id=1, source_target_pairs={{0,1},{1,0},{2,3},{3,2},{4,5},{5,4},{6,7},{7,6},{8,9},{9,8},{10,11... | collective-permute-start | bytes 3848 | tf_op jit(solution)/shard_map/while/body/eval_jaxpr/ppermute | solution.py:25
  250.0 21.0 %collective-permute-start.6 = (f32[16,20]{0,1:T(8,128)}, f32[16,20]{0,1:T(8,128)}, u32[]{:S(2)}, u32[]{:S(2)}) collective-permute-start(f32[16,20]{0,1:T(8,128)} %copy.130), channel_id=1, source_target_pairs={{0,1},{1,0},{2,3},{3,2},{4,5},{5,4},{6,7},{7,6},{8,9},{9,8},{10,11... | collective-permute-start | bytes 3848 | tf_op jit(solution)/shard_map/while/body/eval_jaxpr/ppermute | solution.py:25
  257.8 13.3 %collective-permute-start.7 = (f32[16,1280]{1,0:T(8,128)S(1)}, f32[16,1280]{1,0:T(8,128)S(1)}, u32[]{:S(2)}, u32[]{:S(2)}) collective-permute-start(f32[16,1280]{1,0:T(8,128)S(1)} %add.1613), channel_id=1, source_target_pairs={{0,1},{1,0},{2,3},{3,2},{4,5},{5,4},{6,7},{7,6},{8,9},{9,8},{10,11... | collective-permute-start | bytes 245768 | tf_op jit(solution)/shard_map/while/body/eval_jaxpr/ppermute | solution.py:25
  283.3 214.8 %all-reduce.3.cloned.1.call-start = ((), (), s32[]{:S(2)}) async-start(), calls=%async_computation.1 | async-start | bytes 327680 | tf_op jit(solution)/shard_map/psum | solution.py:214
  297.5 123.4 %collective-permute-start.26 = (f32[1,15,1280]{2,1,0:T(8,128)S(1)}, f32[1,15,1280]{2,1,0:T(8,128)S(1)}, u32[]{:S(2)}, u32[]{:S(2)}) collective-permute-start(f32[1,15,1280]{2,1,0:T(8,128)S(1)} %get-tuple-element.343), channel_id=1, source_target_pairs={{0,1},{2,3},{4,5},{6,7},{8,9},{10,11},{12,13},{14,15},{16,17},{18,... | collective-permute-start | bytes 230408 | tf_op jit(solution)/shard_map/ppermute | solution.py:14
  301.1 119.8 %collective-permute-start.25 = (f32[1,15,1280]{2,1,0:T(8,128)S(1)}, f32[1,15,1280]{2,1,0:T(8,128)S(1)}, u32[]{:S(2)}, u32[]{:S(2)}) collective-permute-start(f32[1,15,1280]{2,1,0:T(8,128)S(1)} %get-tuple-element.342), channel_id=1, source_target_pairs={{1,0},{3,2},{5,4},{7,6},{9,8},{11,10},{13,12},{15,14},{17,16},{19,... | collective-permute-start | bytes 230408 | tf_op jit(solution)/shard_map/ppermute | solution.py:17
  315.1 222.2 %all-reduce.5.cloned.1.call-start = ((), (), s32[]{:S(2)}) async-start(), calls=%async_computation.3 | async-start | bytes 1638400 | tf_op jit(solution)/shard_map/psum | solution.py:223
  (84 other events, 4204.7 us)
Sparse Core Ops, SparseCore 0:
  283.4 137.4 reduce-scatter.1
Sparse Core Ops, SparseCore 1:
  315.2 182.9 all-reduce.2
  500.4 36.8 all-reduce.4
